TPU v7x, 128 devices: a whole 4x4x4 slice. The times are simulated.
128 devices in a mesh: seq: 16 (over z, x), head: 8 (over y, core).
Axes of the slice: x: 4, y: 4, z: 4, core: 2. Of those that a mesh axis runs over, the one named last changes fastest.
Arguments:
- teacher_query: bfloat16 [2, 4096, 8192], P(None, ('seq', 'head')), may hold values from -6 to 6
- student_query: bfloat16 [2, 4096, 8192], P(None, ('seq', 'head')), may hold values from -6 to 6
- kept_heads: int32 [40], replicated, may hold values from 0 to 63, as said below
Outputs:
- relation_loss: float32 [2, 64, 4096], P(None, 'head', 'seq')
Inputs may be any that keep to these rules, and one draw needn't show every extreme that they name: `kept_heads`: the 40 entries are distinct, and 0 and 63 are among them.
All inputs are finite; a program needn't handle non-finite values.
Results may differ from a plain program's by a relative error of at most 0.0003.
Values may be sent and summed in bfloat16 or wider, within the bound.
A program may use at most 128 MiB of HBM per device.

v0:
```python
import jax
import jax.numpy as jnp
from jax import lax
from jax.sharding import PartitionSpec as P

HEADS = 64
HD = 128
KEPT = 40
RELH = 64
TREL = 128
SREL = 80


NEG_FILL = -1e30


def fresh_stats(head_count, query_count):
    lowest = jnp.full((head_count, query_count), NEG_FILL, jnp.float32)
    zeros_block = jnp.zeros((head_count, query_count), jnp.float32)
    return (lowest, zeros_block, zeros_block, lowest, zeros_block)


def relation_update(running, query_pair, key_pair, query_pos, key_pos, scales):
    top_t, total_t, cross_sum, top_s, total_s = running
    teach_scores = (
        jnp.einsum("qhd,khd->hqk", query_pair[0], key_pair[0], preferred_element_type=jnp.float32)
        * scales[0]
    )
    stud_scores = (
        jnp.einsum("qhd,khd->hqk", query_pair[1], key_pair[1], preferred_element_type=jnp.float32)
        * scales[1]
    )
    allowed = key_pos[None, :] <= query_pos[:, None]
    teach_scores = jnp.where(allowed[None], teach_scores, NEG_FILL)
    stud_scores = jnp.where(allowed[None], stud_scores, NEG_FILL)
    new_top_t = jnp.maximum(top_t, jnp.max(teach_scores, axis=2))
    new_top_s = jnp.maximum(top_s, jnp.max(stud_scores, axis=2))
    weights_t = jnp.exp(teach_scores - new_top_t[:, :, None])
    weights_s = jnp.exp(stud_scores - new_top_s[:, :, None])
    decay_t = jnp.exp(top_t - new_top_t)
    decay_s = jnp.exp(top_s - new_top_s)
    total_t = total_t * decay_t + jnp.sum(weights_t, axis=2)
    cross_sum = cross_sum * decay_t + jnp.sum(weights_t * (teach_scores - stud_scores), axis=2)
    total_s = total_s * decay_s + jnp.sum(weights_s, axis=2)
    return (new_top_t, total_t, cross_sum, new_top_s, total_s)


def finish_rows(running):
    top_t, total_t, cross_sum, top_s, total_s = running
    return cross_sum / total_t - top_t - jnp.log(total_t) + top_s + jnp.log(total_s)


def fold_keys(running, query_pair, query_pos, key_pair, last_query, scales):
    key_length = key_pair[0].shape[0]
    key_block = 512
    steps_total = key_length // key_block

    def one_block(block_number, current):
        row_start = block_number * key_block
        block_t = lax.dynamic_slice_in_dim(key_pair[0], row_start, key_block, 0)
        block_s = lax.dynamic_slice_in_dim(key_pair[1], row_start, key_block, 0)
        key_pos = row_start + jnp.arange(key_block, dtype=jnp.int32)
        return relation_update(current, query_pair, (block_t, block_s), query_pos, key_pos, scales)

    needed = jnp.clip(last_query // key_block + 1, 0, steps_total)
    return lax.fori_loop(0, needed, one_block, running)


def batch_inside(local, head_count, width):
    seq_count_b, rows, columns = local.shape
    folded = local.reshape(seq_count_b, rows, head_count, width)
    return jnp.transpose(folded, (1, 0, 2, 3)).reshape(rows, seq_count_b * head_count * width)


def shards(teacher_query, student_query, kept_heads):
    batch_count = student_query.shape[0]
    token_rows = student_query.shape[1]
    split_heads = student_query.reshape(batch_count, token_rows, HEADS, HD)
    picked = jnp.take(split_heads, kept_heads, axis=2).reshape(batch_count, token_rows, KEPT * HD)
    teach_local, stud_local = (
        lax.all_to_all(teacher_query, "head", split_axis=2, concat_axis=1, tiled=True),
        lax.all_to_all(picked, "head", split_axis=2, concat_axis=1, tiled=True),
    )
    local_rows = teach_local.shape[1]
    head_count = RELH // lax.axis_size("head")
    wide_heads = batch_count * head_count
    teach_flat = batch_inside(teach_local, head_count, TREL)
    stud_flat = batch_inside(stud_local, head_count, SREL)
    position = lax.axis_index("seq")
    scales = (TREL ** (-0.5), SREL ** (-0.5))
    teach_heads = teach_flat.reshape(local_rows, wide_heads, TREL)
    stud_heads = stud_flat.reshape(local_rows, wide_heads, SREL)
    query_pos = position * local_rows + jnp.arange(local_rows, dtype=jnp.int32)
    last_query = position * local_rows + local_rows - 1
    key_pair = (
        lax.all_gather(teach_flat, "seq", axis=0, tiled=True).reshape(-1, wide_heads, TREL),
        lax.all_gather(stud_flat, "seq", axis=0, tiled=True).reshape(-1, wide_heads, SREL),
    )
    running = fold_keys(
        fresh_stats(wide_heads, local_rows),
        (teach_heads, stud_heads),
        query_pos,
        key_pair,
        last_query,
        scales,
    )
    return finish_rows(running).reshape(batch_count, head_count, local_rows)


def solution(mesh):
    placed = (P(None, ("seq", "head"), None), P(None, ("seq", "head"), None), P())
    return jax.shard_map(
        shards, mesh=mesh, in_specs=placed, out_specs=P(None, "head", "seq"), check_vma=False
    )
```

profile of v0, /device:TPU:100, one launch (start us, length us, event | category | flops | bytes accessed | tf_op | source)
XLA Modules:
  0.0 360.5 jit_solution(5775087227252518745)
XLA Ops:
  13.1 6.3 %reshape.85 = bf16[8,2,20480]{2,1,0:T(2,128)(2,1)S(1)} reshape(bf16[5120,2,32]{2,1,0:T(2,128)(2,1)} %bitcast.79) | data formatting | bytes 1310720
  19.4 16.1 %all_to_all.30 = bf16[8,2,20480]{2,1,0:T(2,128)(2,1)S(1)} all-to-all(bf16[8,2,20480]{2,1,0:T(2,128)(2,1)S(1)} %reshape.85), channel_id=1, replica_groups=mesh['seq'=16,'head'=8] {'head'}, dimensions={0} | all-to-all | bytes 1310720 | tf_op jit(solution)/shard_map/all_to_all | solution.py:82
  37.8 4.9 %copy.32 = bf16[2,32,8,640]{3,1,2,0:T(8,128)(2,1)S(1)} copy(bf16[2,32,8,640]{1,0,3,2:T(2,128)(2,1)} %bitcast.80) | data formatting | bytes 1310720 | tf_op jit(solution)/shard_map/all_to_all | solution.py:82
  45.2 6.8 %copy.18 = bf16[2,32,8192]{1,0,2:T(2,128)(2,1)} copy(bf16[2,32,8192]{2,1,0:T(8,128)(2,1)S(1)} %copy-done.3) | data formatting | bytes 2097152 | tf_op args[0]
  52.0 7.0 %reshape.83 = bf16[8,2,32768]{2,1,0:T(2,128)(2,1)S(1)} reshape(bf16[8192,2,32]{2,1,0:T(2,128)(2,1)} %bitcast.78) | data formatting | bytes 2097152
  59.1 18.5 %all_to_all.31 = bf16[8,2,32768]{2,1,0:T(2,128)(2,1)S(1)} all-to-all(bf16[8,2,32768]{2,1,0:T(2,128)(2,1)S(1)} %reshape.83), channel_id=1, replica_groups=mesh['seq'=16,'head'=8] {'head'}, dimensions={0} | all-to-all | bytes 2097152 | tf_op jit(solution)/shard_map/all_to_all | solution.py:81
  77.6 4.5 %reshape.84 = bf16[8192,2,32]{2,1,0:T(2,128)(2,1)} reshape(bf16[8,2,32768]{2,1,0:T(2,128)(2,1)S(1)} %all_to_all.31) | data formatting | bytes 2097152
  82.1 9.1 %copy.19 = bf16[2,32,8,1024]{3,1,2,0:T(8,128)(2,1)S(1)} copy(bf16[2,32,8,1024]{1,0,3,2:T(2,128)(2,1)} %bitcast.77) | data formatting | bytes 2097152 | tf_op jit(solution)/shard_map/all_to_all | solution.py:81
  93.5 38.1 %all-gather.5.cloned.1.call-done = bf16[4096,1280]{0,1:T(8,128)(2,1)} async-done(((bf16[256,1280]{0,1:T(8,128)(2,1)}), bf16[4096,1280]{0,1:T(8,128)(2,1)}) %all-gather.5.cloned.1.call-update) | async-done | bytes 10485776 | tf_op jit(solution)/shard_map/all_gather | solution.py:97
  131.6 122.6 %all-gather.3.cloned.1.call-done = bf16[4096,2048]{0,1:T(8,128)(2,1)} async-done(((bf16[256,2048]{0,1:T(8,128)(2,1)}), bf16[4096,2048]{0,1:T(8,128)(2,1)}) %all-gather.3.cloned.1.call-update) | async-done | bytes 16777232 | tf_op jit(solution)/shard_map/all_gather | solution.py:96
  254.2 98.2 %while.19 = (s32[]{:T(128)}, f32[16,256]{1,0:T(8,128)S(1)}, f32[16,256]{1,0:T(8,128)S(1)}, f32[16,256]{1,0:T(8,128)S(1)}, f32[16,256]{1,0:T(8,128)S(1)}, /*index...) while((s32[]{:T(128)}, f32[16,256]{1,0:T(8,128)S(1)}, ...), condition=%wide.region_6.7_spmd.clone, body=%wide.region_0.6_spmd.clone.sunk | while | flops 908219136 | bytes 47945936 | solution.py:66
  257.5 4.4 %fusion.24 = (f32[16,256]{1,0:T(8,128)S(1)}, f32[16,256]{1,0:T(8,128)S(1)}, f32[16,512,256]{2,1,0:T(8,128)S(1)}) fusion(pred[256,512]{0,1:T(8,128)(4,1)S(1)} %broadcast_compare_fusion.2, f32[16,512,256]{2,1,0:T(8,128)S(1)} %fusion.23, bf16[256,16,80]{0,2,1:T(8,128)(2,1)S(1)} %get-tuple-element.308, bf16[4096,16,80]{0,2,1:T(8,128)(2,1)} %get-tuple-element.307, ...), kind=kOutput, calls=%fused_computation.9.clone.1 | convolution fusion | flops 348119040 | bytes 18907140 | tf_op jit(solution)/shard_map/while/body/qhd,khd->hqk/dot_general | solution.py:30
  261.9 4.6 %multiply_reduce_fusion.2 = (f32[16,256]{1,0:T(8,128)S(1)}, f32[16,256]{1,0:T(8,128)S(1)}, f32[16,256]{1,0:T(8,128)S(1)}) fusion(f32[16,512,256]{2,1,0:T(8,128)S(1)} %fusion.23, f32[16,512,256]{2,1,0:T(8,128)S(1)} %get-tuple-element.258, f32[16,256]{1,0:T(8,128)S(1)} %max.15, pred[256,512]{0,1:T(8,128)(4,1)S(1)} %broadcast_compare_fusion.2, ...), kind=kLoop, calls=%fused_computation.5.clone.1 | loop fusion | flops 23056384 | bytes 16990208 | tf_op jit(solution)/shard_map/while/body/reduce_sum | solution.py:43
  269.7 4.4 %fusion.24 = (f32[16,256]{1,0:T(8,128)S(1)}, f32[16,256]{1,0:T(8,128)S(1)}, f32[16,512,256]{2,1,0:T(8,128)S(1)}) fusion(pred[256,512]{0,1:T(8,128)(4,1)S(1)} %broadcast_compare_fusion.2, f32[16,512,256]{2,1,0:T(8,128)S(1)} %fusion.23, bf16[256,16,80]{0,2,1:T(8,128)(2,1)S(1)} %get-tuple-element.308, bf16[4096,16,80]{0,2,1:T(8,128)(2,1)} %get-tuple-element.307, ...), kind=kOutput, calls=%fused_computation.9.clone.1 | convolution fusion | flops 348119040 | bytes 18907140 | tf_op jit(solution)/shard_map/while/body/qhd,khd->hqk/dot_general | solution.py:30
  274.2 4.6 %multiply_reduce_fusion.2 = (f32[16,256]{1,0:T(8,128)S(1)}, f32[16,256]{1,0:T(8,128)S(1)}, f32[16,256]{1,0:T(8,128)S(1)}) fusion(f32[16,512,256]{2,1,0:T(8,128)S(1)} %fusion.23, f32[16,512,256]{2,1,0:T(8,128)S(1)} %get-tuple-element.258, f32[16,256]{1,0:T(8,128)S(1)} %max.15, pred[256,512]{0,1:T(8,128)(4,1)S(1)} %broadcast_compare_fusion.2, ...), kind=kLoop, calls=%fused_computation.5.clone.1 | loop fusion | flops 23056384 | bytes 16990208 | tf_op jit(solution)/shard_map/while/body/reduce_sum | solution.py:43
  286.4 4.6 %multiply_reduce_fusion.2 = (f32[16,256]{1,0:T(8,128)S(1)}, f32[16,256]{1,0:T(8,128)S(1)}, f32[16,256]{1,0:T(8,128)S(1)}) fusion(f32[16,512,256]{2,1,0:T(8,128)S(1)} %fusion.23, f32[16,512,256]{2,1,0:T(8,128)S(1)} %get-tuple-element.258, f32[16,256]{1,0:T(8,128)S(1)} %max.15, pred[256,512]{0,1:T(8,128)(4,1)S(1)} %broadcast_compare_fusion.2, ...), kind=kLoop, calls=%fused_computation.5.clone.1 | loop fusion | flops 23056384 | bytes 16990208 | tf_op jit(solution)/shard_map/while/body/reduce_sum | solution.py:43
  294.2 4.4 %fusion.24 = (f32[16,256]{1,0:T(8,128)S(1)}, f32[16,256]{1,0:T(8,128)S(1)}, f32[16,512,256]{2,1,0:T(8,128)S(1)}) fusion(pred[256,512]{0,1:T(8,128)(4,1)S(1)} %broadcast_compare_fusion.2, f32[16,512,256]{2,1,0:T(8,128)S(1)} %fusion.23, bf16[256,16,80]{0,2,1:T(8,128)(2,1)S(1)} %get-tuple-element.308, bf16[4096,16,80]{0,2,1:T(8,128)(2,1)} %get-tuple-element.307, ...), kind=kOutput, calls=%fused_computation.9.clone.1 | convolution fusion | flops 348119040 | bytes 18907140 | tf_op jit(solution)/shard_map/while/body/qhd,khd->hqk/dot_general | solution.py:30
  298.7 4.6 %multiply_reduce_fusion.2 = (f32[16,256]{1,0:T(8,128)S(1)}, f32[16,256]{1,0:T(8,128)S(1)}, f32[16,256]{1,0:T(8,128)S(1)}) fusion(f32[16,512,256]{2,1,0:T(8,128)S(1)} %fusion.23, f32[16,512,256]{2,1,0:T(8,128)S(1)} %get-tuple-element.258, f32[16,256]{1,0:T(8,128)S(1)} %max.15, pred[256,512]{0,1:T(8,128)(4,1)S(1)} %broadcast_compare_fusion.2, ...), kind=kLoop, calls=%fused_computation.5.clone.1 | loop fusion | flops 23056384 | bytes 16990208 | tf_op jit(solution)/shard_map/while/body/reduce_sum | solution.py:43
  311.0 4.6 %multiply_reduce_fusion.2 = (f32[16,256]{1,0:T(8,128)S(1)}, f32[16,256]{1,0:T(8,128)S(1)}, f32[16,256]{1,0:T(8,128)S(1)}) fusion(f32[16,512,256]{2,1,0:T(8,128)S(1)} %fusion.23, f32[16,512,256]{2,1,0:T(8,128)S(1)} %get-tuple-element.258, f32[16,256]{1,0:T(8,128)S(1)} %max.15, pred[256,512]{0,1:T(8,128)(4,1)S(1)} %broadcast_compare_fusion.2, ...), kind=kLoop, calls=%fused_computation.5.clone.1 | loop fusion | flops 23056384 | bytes 16990208 | tf_op jit(solution)/shard_map/while/body/reduce_sum | solution.py:43
  318.7 4.4 %fusion.24 = (f32[16,256]{1,0:T(8,128)S(1)}, f32[16,256]{1,0:T(8,128)S(1)}, f32[16,512,256]{2,1,0:T(8,128)S(1)}) fusion(pred[256,512]{0,1:T(8,128)(4,1)S(1)} %broadcast_compare_fusion.2, f32[16,512,256]{2,1,0:T(8,128)S(1)} %fusion.23, bf16[256,16,80]{0,2,1:T(8,128)(2,1)S(1)} %get-tuple-element.308, bf16[4096,16,80]{0,2,1:T(8,128)(2,1)} %get-tuple-element.307, ...), kind=kOutput, calls=%fused_computation.9.clone.1 | convolution fusion | flops 348119040 | bytes 18907140 | tf_op jit(solution)/shard_map/while/body/qhd,khd->hqk/dot_general | solution.py:30
  323.2 4.6 %multiply_reduce_fusion.2 = (f32[16,256]{1,0:T(8,128)S(1)}, f32[16,256]{1,0:T(8,128)S(1)}, f32[16,256]{1,0:T(8,128)S(1)}) fusion(f32[16,512,256]{2,1,0:T(8,128)S(1)} %fusion.23, f32[16,512,256]{2,1,0:T(8,128)S(1)} %get-tuple-element.258, f32[16,256]{1,0:T(8,128)S(1)} %max.15, pred[256,512]{0,1:T(8,128)(4,1)S(1)} %broadcast_compare_fusion.2, ...), kind=kLoop, calls=%fused_computation.5.clone.1 | loop fusion | flops 23056384 | bytes 16990208 | tf_op jit(solution)/shard_map/while/body/reduce_sum | solution.py:43
  335.5 4.6 %multiply_reduce_fusion.2 = (f32[16,256]{1,0:T(8,128)S(1)}, f32[16,256]{1,0:T(8,128)S(1)}, f32[16,256]{1,0:T(8,128)S(1)}) fusion(f32[16,512,256]{2,1,0:T(8,128)S(1)} %fusion.23, f32[16,512,256]{2,1,0:T(8,128)S(1)} %get-tuple-element.258, f32[16,256]{1,0:T(8,128)S(1)} %max.15, pred[256,512]{0,1:T(8,128)(4,1)S(1)} %broadcast_compare_fusion.2, ...), kind=kLoop, calls=%fused_computation.5.clone.1 | loop fusion | flops 23056384 | bytes 16990208 | tf_op jit(solution)/shard_map/while/body/reduce_sum | solution.py:43
  343.3 4.4 %fusion.24 = (f32[16,256]{1,0:T(8,128)S(1)}, f32[16,256]{1,0:T(8,128)S(1)}, f32[16,512,256]{2,1,0:T(8,128)S(1)}) fusion(pred[256,512]{0,1:T(8,128)(4,1)S(1)} %broadcast_compare_fusion.2, f32[16,512,256]{2,1,0:T(8,128)S(1)} %fusion.23, bf16[256,16,80]{0,2,1:T(8,128)(2,1)S(1)} %get-tuple-element.308, bf16[4096,16,80]{0,2,1:T(8,128)(2,1)} %get-tuple-element.307, ...), kind=kOutput, calls=%fused_computation.9.clone.1 | convolution fusion | flops 348119040 | bytes 18907140 | tf_op jit(solution)/shard_map/while/body/qhd,khd->hqk/dot_general | solution.py:30
  347.7 4.6 %multiply_reduce_fusion.2 = (f32[16,256]{1,0:T(8,128)S(1)}, f32[16,256]{1,0:T(8,128)S(1)}, f32[16,256]{1,0:T(8,128)S(1)}) fusion(f32[16,512,256]{2,1,0:T(8,128)S(1)} %fusion.23, f32[16,512,256]{2,1,0:T(8,128)S(1)} %get-tuple-element.258, f32[16,256]{1,0:T(8,128)S(1)} %max.15, pred[256,512]{0,1:T(8,128)(4,1)S(1)} %broadcast_compare_fusion.2, ...), kind=kLoop, calls=%fused_computation.5.clone.1 | loop fusion | flops 23056384 | bytes 16990208 | tf_op jit(solution)/shard_map/while/body/reduce_sum | solution.py:43
  (109 shorter events, 52.8 us)
Async XLA Ops:
  6.5 1.5 copy-start
  6.5 125.1 %all-gather.5.cloned.1.call-start = ((), (), s32[]{:S(2)}) async-start(), calls=%async_computation.3 | async-start | bytes 11141120 | tf_op jit(solution)/shard_map/all_gather | solution.py:97
  13.1 32.1 %copy-start.3 = (bf16[2,32,8192]{2,1,0:T(8,128)(2,1)S(1)}, bf16[2,32,8192]{2,1,0:T(8,128)(2,1)}, u32[]{:S(2)}) copy-start(bf16[2,32,8192]{2,1,0:T(8,128)(2,1)} %param.5) | copy-start | bytes 3145732
  45.1 209.0 %all-gather.3.cloned.1.call-start = ((), (), s32[]{:S(2)}) async-start(), calls=%async_computation.2 | async-start | bytes 17825792 | tf_op jit(solution)/shard_map/all_gather | solution.py:96
  82.1 172.1 %copy-start.2 = (bf16[256,2,8,80]{0,3,2,1:T(8,128)(2,1)S(1)}, bf16[256,2,8,80]{0,3,2,1:T(8,128)(2,1)}, u32[]{:S(2)}) copy-start(bf16[256,2,8,80]{0,3,2,1:T(8,128)(2,1)} %copy.27) | copy-start | bytes 1966084
  352.4 1.2 copy-start.1
Sparse Core Ops, SparseCore 0:
  45.3 86.2 all-gather.4
  133.7 120.4 all-gather.2
where the time goes:
time: 362 us; the launch traced here: 361 us
  waiting for transfers between devices  161 us (44%)
  matrix products  58.5 us (16%)
  local copies, waits for them, and re-layouts  51.3 us (14%)
  other arithmetic  40.8 us (11%)
  blocking collectives  34.6 us (10%)
  between operations  13.6 us (4%)
    all_gather x1, waiting for transfers between devices, shards(): lax.all_gather(teach_flat, 'seq', axis=0, tiled=True)  123 us
    all_gather x1, waiting for transfers between devices, shards(): lax.all_gather(stud_flat, 'seq', axis=0, tiled=True)  38.1 us
    reduce_sum x8, other arithmetic, relation_update(): jnp.sum(weights_t * (teach_scores - stud_scores), axis=2)  37.2 us
    dot_general x8, matrix products, relation_update(): jnp.einsum('qhd,khd->hqk', query_pair[1], key_pair[1], preferred_element_...  35.4 us
    unnamed x15, local copies, waits for them, and re-layouts  28.1 us
    dot_general x8, matrix products, relation_update(): jnp.einsum('qhd,khd->hqk', query_pair[0], key_pair[0], preferred_element_...  23.2 us
    all_to_all x1, blocking collectives, shards(): lax.all_to_all(teacher_query, 'head', split_axis=2, concat_axis=1, tiled=...  18.5 us
    all_to_all x1, blocking collectives, shards(): lax.all_to_all(picked, 'head', split_axis=2, concat_axis=1, tiled=True)  16.1 us
  transfers between devices with their start and end apart: 2, of which 2 were waited for; matrix products, arithmetic and copies ran while one was open for 8% of the time, Pallas kernels for 0%

commit v1 on v0

v1 whole, which is shorter than its diff:
```python
import functools
import math

import jax
import jax.numpy as jnp
from jax import lax
from jax.experimental import pallas as pl
from jax.experimental.pallas import tpu as pltpu
from jax.sharding import PartitionSpec as P

HEADS = 64
HD = 128
KEPT = 40
RELH = 64
TREL = 128
SREL = 80

MESH = pl.DeviceIdType.MESH
BF = jnp.bfloat16
F32 = jnp.float32

SCALE_T = math.log2(math.e) / math.sqrt(TREL)
SCALE_S = math.log2(math.e) / math.sqrt(SREL)
OFFSET = 60.0


def params(mesh):
    return mesh.shape["seq"], mesh.shape["head"]


def kernel(
    seq_n, head_n, rows, chunk,
    kept_ref, teach_hbm, stud_hbm, out_ref,
    stud_in, stud_out, tea, stu, tea_shift, stu_query, sums, rows_out, rows_in,
    in_sem, send_t, send_s, recv_t, recv_s, send_o, recv_o,
):
    total = seq_n * head_n
    seq_me = lax.axis_index("seq")
    head_me = lax.axis_index("head")
    me = seq_me * head_n + head_me
    positions = rows * total
    chunks = positions // chunk
    per_chunk = chunk // rows
    my_chunk = me // per_chunk

    def place(t):
        return (t // head_n, lax.rem(t, head_n))

    @pl.loop(0, HEADS)
    def _(i):
        head = stud_hbm.at[:, :, pl.ds(pl.multiple_of(i * HD, HD), HD)]
        pltpu.make_async_copy(head, stud_in.at[i], in_sem).start()

    barrier = pltpu.get_barrier_semaphore()

    @pl.loop(1, total)
    def _(k):
        pl.semaphore_signal(barrier, inc=1, device_id=place(lax.rem(me + k, total)), device_id_type=MESH)

    sums[...] = jnp.zeros_like(sums)
    pltpu.make_async_copy(stud_in, stud_in, in_sem).wait()

    lane = lax.broadcasted_iota(jnp.int32, (rows, HD), 1)

    @pl.loop(0, 2 * head_n)
    def _(bg):
        b = bg // head_n
        g = lax.rem(bg, head_n)
        heads = [stud_in[kept_ref[5 * g + i], b].astype(F32) for i in range(5)]
        for u in range(8):
            first = (u * SREL) // HD
            offset = (u * SREL) % HD
            piece = heads[first]
            if offset:
                piece = pltpu.roll(piece, HD - offset, 1)
            if offset + SREL > HD:
                other = pltpu.roll(heads[first + 1], HD - offset, 1)
                piece = jnp.where(lane < HD - offset, piece, other)
            piece = jnp.where(lane < SREL, piece, jnp.where(lane == SREL, 1.0, 0.0))
            stud_out[(b * 8 + u) * head_n + g] = piece.astype(BF)

    pl.semaphore_wait(barrier, total - 1)

    mine = pl.ds(pl.multiple_of(me * rows, rows), rows)

    def teach_src(t):
        s, h = place(t)
        r = h * 8 + lax.rem(s, 8)
        return teach_hbm.at[s // 8, :, pl.ds(pl.multiple_of(r * TREL, TREL), TREL)]

    own_t = pltpu.make_async_copy(teach_src(me), tea.at[mine], recv_t.at[my_chunk])
    own_s = pltpu.make_async_copy(stud_out.at[me], stu.at[mine], recv_s.at[my_chunk])
    own_t.start()
    own_s.start()

    @pl.loop(1, total)
    def _(k):
        t = lax.rem(me + k, total)
        pltpu.make_async_remote_copy(
            src_ref=teach_src(t), dst_ref=tea.at[mine], send_sem=send_t, recv_sem=recv_t.at[my_chunk],
            device_id=place(t), device_id_type=MESH,
        ).start()
        pltpu.make_async_remote_copy(
            src_ref=stud_out.at[t], dst_ref=stu.at[mine], send_sem=send_s, recv_sem=recv_s.at[my_chunk],
            device_id=place(t), device_id_type=MESH,
        ).start()

    half = chunk // 2
    row_i = lax.broadcasted_iota(jnp.int32, (TREL, HD), 0)
    col_i = lax.broadcasted_iota(jnp.int32, (TREL, HD), 1)
    pick_t = jnp.where(col_i == 0, 1.0, 0.0).astype(BF)
    pick_s = jnp.where((col_i == SREL) & (row_i < SREL), 1.0, 0.0).astype(BF)
    chunk_lane = lax.broadcasted_iota(jnp.int32, (chunk, HD), 1)
    ones_t = jnp.where(chunk_lane == 0, 1.0, 0.0).astype(BF)

    def rows_dot(x, y):
        return lax.dot_general(x, y, (((1,), (1,)), ((), ())), preferred_element_type=F32)

    def tile(key_start, key_count, query_start, masked):
        keys = pl.ds(pl.multiple_of(key_start, half), key_count)
        queries = pl.ds(pl.multiple_of(query_start, half), half)
        key_t = jnp.concatenate([tea[keys], ones_t[:key_count]], axis=1)
        key_s = stu[keys]
        key_s = jnp.concatenate([key_s, key_s], axis=1)
        query_t = jnp.concatenate([tea[queries], tea_shift[queries]], axis=1)
        query_s = stu_query[queries]
        score_t = rows_dot(key_t, query_t) * SCALE_T
        score_s = rows_dot(key_s, query_s)
        if masked:
            key_i = lax.broadcasted_iota(jnp.int32, (key_count, half), 0)
            query_i = lax.broadcasted_iota(jnp.int32, (key_count, half), 1)
            seen = key_i <= query_i + (key_count - half)
            score_t = jnp.where(seen, score_t, -1e30)
            score_s = jnp.where(seen, score_s, -1e30)
        weight_t = jnp.exp2(score_t)
        weight_s = jnp.exp2(score_s)
        cross = weight_t * (score_t - score_s)
        fold = lambda x: jnp.sum(x.reshape(key_count // 8, 8, half), axis=0)
        sums[0, :, queries] += fold(weight_t)
        sums[1, :, queries] += fold(weight_s)
        sums[2, :, queries] += fold(cross)

    @pl.loop(1, chunks + 1)
    def _(n):
        c = lax.rem(my_chunk - n + chunks, chunks)
        here = pl.ds(pl.multiple_of(c * chunk, chunk), chunk)
        pltpu.make_async_copy(tea.at[here], tea.at[here], recv_t.at[c]).wait()
        pltpu.make_async_copy(stu.at[here], stu.at[here], recv_s.at[c]).wait()

        a = tea[here].astype(F32)
        norm_t = jnp.dot((a * a).astype(BF), pick_t, preferred_element_type=F32)
        tea_shift[here] = jnp.where(chunk_lane == 0, -OFFSET / SCALE_T - norm_t, 0.0).astype(BF)
        b = stu[here].astype(F32)
        norm_s = jnp.dot((b * b).astype(BF), pick_s, preferred_element_type=F32)
        scaled = jnp.where(chunk_lane < SREL, b * SCALE_S, 0.0)
        high = scaled.astype(BF)
        low = (scaled - high.astype(F32)).astype(BF)
        high = jnp.where(chunk_lane == SREL, -OFFSET - SCALE_S * norm_s, high.astype(F32)).astype(BF)
        stu_query[here] = jnp.concatenate([high, low], axis=1)

        @pl.loop(1, n)
        def _(m):
            d = lax.rem(my_chunk - m + chunks, chunks)
            upper, lower = jnp.maximum(c, d), jnp.minimum(c, d)
            tile(lower * chunk, chunk, upper * chunk, False)
            tile(lower * chunk, chunk, upper * chunk + half, False)

        tile(c * chunk, half, c * chunk, True)
        tile(c * chunk, chunk, c * chunk + half, True)

    each = positions // seq_n
    for j in range(seq_n):
        part = pl.ds(j * each, each)
        total_t = jnp.sum(sums[0, :, part], axis=0, keepdims=True)
        total_s = jnp.sum(sums[1, :, part], axis=0, keepdims=True)
        cross = jnp.sum(sums[2, :, part], axis=0, keepdims=True)
        rows_out[j] = (cross / total_t - jnp.log2(total_t) + jnp.log2(total_s)) * math.log(2.0)

    own_o = pltpu.make_async_copy(rows_out.at[seq_me], rows_in.at[seq_me], recv_o)
    own_o.start()

    @pl.loop(1, seq_n)
    def _(k):
        s = lax.rem(seq_me + k, seq_n)
        pltpu.make_async_remote_copy(
            src_ref=rows_out.at[s], dst_ref=rows_in.at[seq_me], send_sem=send_o, recv_sem=recv_o,
            device_id=(s, head_me), device_id_type=MESH,
        ).start()

    pltpu.make_async_copy(rows_in, rows_in, recv_o).wait()
    out_ref[...] = rows_in[...].reshape(2, 8, each)

    sent = pl.ds(0, (total - 1) * rows)
    pltpu.make_async_copy(tea.at[sent], tea.at[sent], send_t).wait()
    pltpu.make_async_copy(stu.at[sent], stu.at[sent], send_s).wait()
    others = pl.ds(0, seq_n - 1)
    pltpu.make_async_copy(rows_in.at[others], rows_in.at[others], send_o).wait()


def shards(seq_n, head_n, teacher_query, student_query, kept_heads):
    batch, rows, width = teacher_query.shape
    total = seq_n * head_n
    positions = rows * total
    chunk = 512
    chunks = positions // chunk
    each = positions // seq_n
    vm = pltpu.VMEM
    dma = pltpu.SemaphoreType.DMA
    return pl.pallas_call(
        functools.partial(kernel, seq_n, head_n, rows, chunk),
        out_shape=jax.ShapeDtypeStruct((batch, RELH // head_n, each), F32),
        in_specs=[
            pl.BlockSpec(memory_space=pltpu.SMEM),
            pl.BlockSpec(memory_space=pl.ANY),
            pl.BlockSpec(memory_space=pl.ANY),
        ],
        out_specs=pl.BlockSpec(memory_space=pltpu.VMEM),
        scratch_shapes=[
            vm((HEADS, batch, rows, HD), BF),
            vm((total, rows, HD), BF),
            vm((positions, TREL), BF),
            vm((positions, HD), BF),
            vm((positions, HD), BF),
            vm((positions, 2 * HD), BF),
            vm((3, 8, positions), F32),
            vm((seq_n, 1, each), F32),
            vm((seq_n, 1, each), F32),
            dma, dma, dma, dma((chunks,)), dma((chunks,)), dma, dma,
        ],
        compiler_params=pltpu.CompilerParams(
            collective_id=0, has_side_effects=True, vmem_limit_bytes=48 * 2**20
        ),
    )(kept_heads, teacher_query, student_query)


def solution(mesh):
    seq_n, head_n = params(mesh)
    placed = (P(None, ("seq", "head"), None), P(None, ("seq", "head"), None), P())
    return jax.shard_map(
        functools.partial(shards, seq_n, head_n),
        mesh=mesh, in_specs=placed, out_specs=P(None, "head", "seq"), check_vma=False,
    )
```

time: 362 us -> 69.4 us (0.19)
  the two profiles are of different devices: /device:TPU:100 before, /device:TPU:1 now
where the time goes in v1:
time: 69.4 us; the launch traced here: 69.2 us
  Pallas kernels  65.5 us (94%)
  local copies, waits for them, and re-layouts  3.71 us (5%)
    pallas_call x1, Pallas kernels, shards(): pl.pallas_call(functools.partial(kernel, seq_n, head_n, rows, chunk), out...  65.5 us
    unnamed x7, local copies, waits for them, and re-layouts  3.71 us

profile of v1, /device:TPU:1, one launch (start us, length us, event | category | flops | bytes accessed | tf_op | source)
XLA Modules:
  0.0 69.2 jit_solution(3284458350476322857)
XLA Ops:
  0.0 0.0 copy-start
  0.0 1.2 %copy-done = bf16[2,32,8192]{2,1,0:T(8,128)(2,1)S(1)} copy-done((bf16[2,32,8192]{2,1,0:T(8,128)(2,1)S(1)}, bf16[2,32,8192]{2,1,0:T(8,128)(2,1)}, u32[]{:S(2)}) %copy-start) | copy-done | bytes 1048600
  1.2 0.0 copy-start.1
  1.2 1.2 %copy-done.1 = bf16[2,32,8192]{2,1,0:T(8,128)(2,1)S(1)} copy-done((bf16[2,32,8192]{2,1,0:T(8,128)(2,1)S(1)}, bf16[2,32,8192]{2,1,0:T(8,128)(2,1)}, u32[]{:S(2)}) %copy-start.1) | copy-done | bytes 1048600
  2.5 0.0 copy-start.2
  2.5 0.7 copy-done.2
  3.1 65.5 %shard_map.37 = f32[2,8,256]{2,1,0:T(8,128)S(1)} custom-call(s32[40]{0:T(128)S(1)} %copy-done.2, bf16[2,32,8192]{2,1,0:T(8,128)(2,1)S(1)} %copy-done, bf16[2,32,8192]{2,1,0:T(8,128)(2,1)S(1)} %copy-done.1), custom_call_target="tpu_custom_call" | custom-call | tf_op jit(solution)/shard_map/pallas_call | solution.py:209
  68.6 0.6 copy.5
Async XLA Ops:
  0.0 1.2 %copy-start = (bf16[2,32,8192]{2,1,0:T(8,128)(2,1)S(1)}, bf16[2,32,8192]{2,1,0:T(8,128)(2,1)}, u32[]{:S(2)}) copy-start(bf16[2,32,8192]{2,1,0:T(8,128)(2,1)} %teach_hbm.1) | copy-start | bytes 3145732
  1.2 1.2 %copy-start.1 = (bf16[2,32,8192]{2,1,0:T(8,128)(2,1)S(1)}, bf16[2,32,8192]{2,1,0:T(8,128)(2,1)}, u32[]{:S(2)}) copy-start(bf16[2,32,8192]{2,1,0:T(8,128)(2,1)} %stud_hbm.1) | copy-start | bytes 3145732
  2.5 0.7 copy-start.2

commit v2 on v1

v2 whole, which is shorter than its diff:
```python
import functools
import math

import jax
import jax.numpy as jnp
from jax import lax
from jax.experimental import pallas as pl
from jax.experimental.pallas import tpu as pltpu
from jax.sharding import PartitionSpec as P

HEADS = 64
HD = 128
KEPT = 40
RELH = 64
TREL = 128
SREL = 80

MESH = pl.DeviceIdType.MESH
BF = jnp.bfloat16
F32 = jnp.float32

SCALE_T = math.log2(math.e) / math.sqrt(TREL)
SCALE_S = math.log2(math.e) / math.sqrt(SREL)
OFFSET = 60.0


def params(mesh):
    return mesh.shape["seq"], mesh.shape["head"]


ORDER = (1, 3, 2, 0)
AHEAD = 4


def xor2(a, b):
    bits = [lax.rem(lax.div(a, w) + lax.div(b, w), 2) * w for w in (1, 2)]
    return bits[0] + bits[1]


def kernel(
    seq_n, head_n, rows, chunk,
    kept_ref, teach_hbm, stud_hbm, out_ref,
    teach_in, stud_in, stud_out, packed, tea, stu, tea_shift, stu_query, sums, rows_out, rows_in,
    in_t, in_sem, send_t, send_s, recv_t, recv_s, send_o, recv_o,
):
    total = seq_n * head_n
    seq_me = lax.axis_index("seq")
    head_me = lax.axis_index("head")
    me = seq_me * head_n + head_me
    positions = rows * total
    chunks = positions // chunk
    per_chunk = chunk // rows
    my_chunk = lax.div(seq_me, 4)
    core_me = lax.rem(head_me, 2)
    y_me = lax.div(head_me, 2)
    x_me = lax.rem(seq_me, 4)

    def chunk_at(step, core):
        code = jnp.int32(ORDER[0])
        for i in range(1, chunks):
            code = jnp.where(step == i, ORDER[i], code)
        return xor2(xor2(my_chunk, code), 2 * core)

    barrier = pltpu.get_barrier_semaphore()

    heads_from_me = [lax.rem(head_me + i, head_n) for i in range(head_n)]
    for h in heads_from_me[1:]:
        pl.semaphore_signal(barrier, inc=1, device_id=(seq_me, h), device_id_type=MESH)

    @pl.loop(1, seq_n)
    def _(k):
        s = lax.rem(seq_me + k, seq_n)
        for h in heads_from_me:
            pl.semaphore_signal(barrier, inc=1, device_id=(s, h), device_id_type=MESH)

    @pl.loop(0, HEADS)
    def _(i):
        head = stud_hbm.at[:, :, pl.ds(pl.multiple_of(i * HD, HD), HD)]
        pltpu.make_async_copy(head, stud_in.at[i], in_sem).start()

    load_t = pltpu.make_async_copy(teach_hbm, teach_in, in_t)
    load_t.start()

    sums[...] = jnp.zeros_like(sums)
    pltpu.make_async_copy(stud_in, stud_in, in_sem).wait()

    lane = lax.broadcasted_iota(jnp.int32, (rows, HD), 1)
    tile_lane = lax.broadcasted_iota(jnp.int32, (8, HD), 1)

    @pl.loop(0, 2 * head_n)
    def _(bg):
        b = lax.div(bg, head_n)
        g = lax.rem(bg, head_n)
        heads = [stud_in[kept_ref[5 * g + i], b].astype(F32) for i in range(5)]
        for u in range(8):
            first = (u * SREL) // HD
            offset = (u * SREL) % HD
            piece = heads[first]
            if offset:
                piece = pltpu.roll(piece, HD - offset, 1)
            if offset + SREL > HD:
                other = pltpu.roll(heads[first + 1], HD - offset, 1)
                piece = jnp.where(lane < HD - offset, piece, other)
            v = piece.reshape(4, 8, HD)
            rest = [pltpu.roll(v[i], 64 + 16 * i, 1) for i in range(4)]
            rest = jnp.where(tile_lane < 32, jnp.where(tile_lane < 16, rest[0], rest[1]), jnp.where(tile_lane < 48, rest[2], rest[3]))
            to = (b * 8 + u) * head_n + g
            stud_out[to, 0] = jnp.where(tile_lane < 64, v[0], pltpu.roll(v[2], 64, 1)).astype(BF)
            stud_out[to, 1] = jnp.where(tile_lane < 64, v[1], pltpu.roll(v[3], 64, 1)).astype(BF)
            stud_out[to, 2] = rest.astype(BF)

    load_t.wait()
    pl.semaphore_wait(barrier, total - 1)

    mine = pl.ds(pl.multiple_of(me * rows, rows), rows)

    def teach_src(s, h):
        r = h * 8 + lax.rem(s, 8)
        return teach_in.at[lax.div(s, 8), :, pl.ds(pl.multiple_of(r * TREL, TREL), TREL)]

    own_t = pltpu.make_async_copy(teach_src(seq_me, head_me), tea.at[mine], recv_t.at[my_chunk])
    own_s = pltpu.make_async_copy(stud_out.at[me], packed.at[me], recv_s.at[my_chunk])
    own_t.start()
    own_s.start()

    x_at = [lax.rem(x_me + i, 4) for i in range(4)]
    y_at = [lax.rem(y_me + i, 4) for i in range(4)]

    def send(step):
        chunk_of = [chunk_at(step, core) for core in range(2)]
        for j in range(per_chunk):
            core, x = j % 2, (j // 2) % 4
            y = (x + j // 8) % 4
            s = chunk_of[core] * 4 + x_at[x]
            h = y_at[y] * 2 + core

            def copies(s=s, h=h):
                pltpu.make_async_remote_copy(
                    src_ref=teach_src(s, h), dst_ref=tea.at[mine], send_sem=send_t, recv_sem=recv_t.at[my_chunk],
                    device_id=(s, h), device_id_type=MESH,
                ).start()
                pltpu.make_async_remote_copy(
                    src_ref=stud_out.at[s * head_n + h], dst_ref=packed.at[me], send_sem=send_s,
                    recv_sem=recv_s.at[my_chunk], device_id=(s, h), device_id_type=MESH,
                ).start()

            if x == 0 and y == 0:
                pl.when((s != seq_me) | (h != head_me))(copies)
            else:
                copies()

    @pl.loop(0, AHEAD)
    def _(step):
        send(step)

    part = 256
    row_i = lax.broadcasted_iota(jnp.int32, (TREL, HD), 0)
    col_i = lax.broadcasted_iota(jnp.int32, (TREL, HD), 1)
    pick_t = jnp.where(col_i == 0, 1.0, 0.0).astype(BF)
    pick_s = jnp.where((col_i == SREL) & (row_i < SREL), 1.0, 0.0).astype(BF)
    chunk_lane = lax.broadcasted_iota(jnp.int32, (chunk, HD), 1)
    ones_t = jnp.where(chunk_lane == 0, 1.0, 0.0).astype(BF)

    def rows_dot(x, y):
        return lax.dot_general(x, y, (((1,), (1,)), ((), ())), preferred_element_type=F32)

    def scores(key_start, key_count, query_start):
        keys = pl.ds(pl.multiple_of(key_start, part), key_count)
        queries = pl.ds(pl.multiple_of(query_start, part), part)
        key_t = jnp.concatenate([tea[keys], ones_t[:key_count]], axis=1)
        key_s = stu[keys]
        key_s = jnp.concatenate([key_s, key_s], axis=1)
        query_t = jnp.concatenate([tea[queries], tea_shift[queries]], axis=1)
        return rows_dot(key_t, query_t) * SCALE_T, rows_dot(key_s, stu_query[queries])

    def add(query_start, pairs):
        queries = pl.ds(pl.multiple_of(query_start, part), part)
        fold = lambda x: jnp.sum(x.reshape(-1, 8, part), axis=0)
        for score_t, score_s in pairs:
            weight_t = jnp.exp2(score_t)
            weight_s = jnp.exp2(score_s)
            sums[0, :, queries] += fold(weight_t)
            sums[1, :, queries] += fold(weight_s)
            sums[2, :, queries] += fold(weight_t * (score_t - score_s))

    def below(key_start, query_start):
        for q in range(0, chunk, part):
            add(query_start + q, [scores(key_start, chunk, query_start + q)])

    def diagonal(start):
        key_i = lax.broadcasted_iota(jnp.int32, (part, part), 0)
        query_i = lax.broadcasted_iota(jnp.int32, (part, part), 1)
        seen = key_i <= query_i
        for q in range(0, chunk, part):
            score_t, score_s = scores(start, q + part, start + q)
            pairs = [(jnp.where(seen, score_t[q:], -1e30), jnp.where(seen, score_s[q:], -1e30))]
            if q:
                pairs.append((score_t[:q], score_s[:q]))
            add(start + q, pairs)

    @pl.loop(0, chunks)
    def _(n):
        c = chunk_at(n, core_me)
        here = pl.ds(pl.multiple_of(c * chunk, chunk), chunk)
        pltpu.make_async_copy(tea.at[here], tea.at[here], recv_t.at[c]).wait()
        from_c = pl.ds(pl.multiple_of(c * per_chunk, per_chunk), per_chunk)
        pltpu.make_async_copy(packed.at[from_c], packed.at[from_c], recv_s.at[c]).wait()

        @pl.when(n + AHEAD < chunks)
        def _():
            send(n + AHEAD)

        a = tea[here].astype(F32)
        norm_t = jnp.dot((a * a).astype(BF), pick_t, preferred_element_type=F32)
        tea_shift[here] = jnp.where(chunk_lane == 0, -OFFSET / SCALE_T - norm_t, 0.0).astype(BF)
        u = packed[from_c].astype(F32)
        lanes = lax.broadcasted_iota(jnp.int32, (per_chunk, 8, HD), 2)
        first = [u[:, 0], u[:, 1], pltpu.roll(u[:, 0], 64, 2), pltpu.roll(u[:, 1], 64, 2)]
        b = jnp.stack(
            [jnp.where(lanes < 64, first[i], pltpu.roll(u[:, 2], 64 - 16 * i, 2)) for i in range(4)], axis=1
        ).reshape(chunk, HD)
        b = jnp.where(chunk_lane < SREL, b, 0.0)
        stu[here] = jnp.where(chunk_lane == SREL, 1.0, b).astype(BF)
        norm_s = jnp.dot((b * b).astype(BF), pick_s, preferred_element_type=F32)
        scaled = b * SCALE_S
        high = scaled.astype(BF)
        low = (scaled - high.astype(F32)).astype(BF)
        high = jnp.where(chunk_lane == SREL, -OFFSET - SCALE_S * norm_s, high.astype(F32)).astype(BF)
        stu_query[here] = jnp.concatenate([high, low], axis=1)

        @pl.loop(0, n)
        def _(m):
            d = chunk_at(m, core_me)
            upper, lower = jnp.maximum(c, d), jnp.minimum(c, d)
            below(lower * chunk, upper * chunk)

        diagonal(c * chunk)

    each = positions // seq_n
    for j in range(seq_n):
        part = pl.ds(j * each, each)
        total_t = jnp.sum(sums[0, :, part], axis=0, keepdims=True)
        total_s = jnp.sum(sums[1, :, part], axis=0, keepdims=True)
        cross = jnp.sum(sums[2, :, part], axis=0, keepdims=True)
        rows_out[j] = (cross / total_t - jnp.log2(total_t) + jnp.log2(total_s)) * math.log(2.0)

    own_o = pltpu.make_async_copy(rows_out.at[seq_me], rows_in.at[seq_me], recv_o)
    own_o.start()

    @pl.loop(1, seq_n)
    def _(k):
        s = lax.rem(seq_me + k, seq_n)
        pltpu.make_async_remote_copy(
            src_ref=rows_out.at[s], dst_ref=rows_in.at[seq_me], send_sem=send_o, recv_sem=recv_o,
            device_id=(s, head_me), device_id_type=MESH,
        ).start()

    pltpu.make_async_copy(rows_in, rows_in, recv_o).wait()
    out_ref[...] = rows_in[...].reshape(2, 8, each)

    sent = pl.ds(0, (total - 1) * rows)
    sent_s = pl.ds(0, total - 1)
    pltpu.make_async_copy(tea.at[sent], tea.at[sent], send_t).wait()
    pltpu.make_async_copy(packed.at[sent_s], packed.at[sent_s], send_s).wait()
    others = pl.ds(0, seq_n - 1)
    pltpu.make_async_copy(rows_in.at[others], rows_in.at[others], send_o).wait()


def shards(seq_n, head_n, teacher_query, student_query, kept_heads):
    batch, rows, width = teacher_query.shape
    total = seq_n * head_n
    positions = rows * total
    chunk = 1024
    chunks = positions // chunk
    each = positions // seq_n
    vm = pltpu.VMEM
    dma = pltpu.SemaphoreType.DMA
    return pl.pallas_call(
        functools.partial(kernel, seq_n, head_n, rows, chunk),
        out_shape=jax.ShapeDtypeStruct((batch, RELH // head_n, each), F32),
        in_specs=[
            pl.BlockSpec(memory_space=pltpu.SMEM),
            pl.BlockSpec(memory_space=pltpu.HBM),
            pl.BlockSpec(memory_space=pltpu.HBM),
        ],
        out_specs=pl.BlockSpec(memory_space=pltpu.VMEM),
        scratch_shapes=[
            vm((batch, rows, width), BF),
            vm((HEADS, batch, rows, HD), BF),
            vm((total, 3, 8, HD), BF),
            vm((total, 3, 8, HD), BF),
            vm((positions, TREL), BF),
            vm((positions, HD), BF),
            vm((positions, HD), BF),
            vm((positions, 2 * HD), BF),
            vm((3, 8, positions), F32),
            vm((seq_n, 1, each), F32),
            vm((seq_n, 1, each), F32),
            dma, dma, dma, dma, dma((chunks,)), dma((chunks,)), dma, dma,
        ],
        compiler_params=pltpu.CompilerParams(
            collective_id=0, has_side_effects=True, vmem_limit_bytes=48 * 2**20
        ),
    )(kept_heads, teacher_query, student_query)


def solution(mesh):
    seq_n, head_n = params(mesh)
    placed = (P(None, ("seq", "head"), None), P(None, ("seq", "head"), None), P())
    return jax.shard_map(
        functools.partial(shards, seq_n, head_n),
        mesh=mesh, in_specs=placed, out_specs=P(None, "head", "seq"), check_vma=False,
    )
```

time: 69.4 us -> 50.5 us (0.73)
  Pallas kernels: 65.5 us -> 46.6 us
    pallas_call x1, Pallas kernels: 65.5 us -> 46.6 us  [shards(): pl.pallas_call(functools.partial(kernel, seq_n, head_n, rows, chunk), out...]
where the time goes in v2:
time: 50.5 us; the launch traced here: 50.3 us
  Pallas kernels  46.6 us (92%)
  local copies, waits for them, and re-layouts  3.71 us (7%)
    pallas_call x1, Pallas kernels, shards(): pl.pallas_call(functools.partial(kernel, seq_n, head_n, rows, chunk), out...  46.6 us
    unnamed x7, local copies, waits for them, and re-layouts  3.71 us

profile of v2, /device:TPU:1, one launch (start us, length us, event | category | flops | bytes accessed | tf_op | source)
XLA Modules:
  0.0 50.3 jit_solution(12204001161831006706)
XLA Ops:
  0.0 0.0 copy-start
  0.0 1.2 %copy-done = bf16[2,32,8192]{2,1,0:T(8,128)(2,1)S(1)} copy-done((bf16[2,32,8192]{2,1,0:T(8,128)(2,1)S(1)}, bf16[2,32,8192]{2,1,0:T(8,128)(2,1)}, u32[]{:S(2)}) %copy-start) | copy-done | bytes 1048600
  1.2 0.0 copy-start.1
  1.2 1.2 %copy-done.1 = bf16[2,32,8192]{2,1,0:T(8,128)(2,1)S(1)} copy-done((bf16[2,32,8192]{2,1,0:T(8,128)(2,1)S(1)}, bf16[2,32,8192]{2,1,0:T(8,128)(2,1)}, u32[]{:S(2)}) %copy-start.1) | copy-done | bytes 1048600
  2.5 0.0 copy-start.2
  2.5 0.7 %copy-done.2 = s32[40]{0:T(128)S(1)} copy-done((s32[40]{0:T(128)S(1)}, s32[40]{0:T(128)}, u32[]{:S(2)}) %copy-start.2) | copy-done | bytes 184
  3.1 46.6 %shard_map.37 = f32[2,8,256]{2,1,0:T(8,128)S(1)} custom-call(s32[40]{0:T(128)S(1)} %copy-done.2, bf16[2,32,8192]{2,1,0:T(8,128)(2,1)S(1)} %copy-done, bf16[2,32,8192]{2,1,0:T(8,128)(2,1)S(1)} %copy-done.1), custom_call_target="tpu_custom_call" | custom-call | tf_op jit(solution)/shard_map/pallas_call | solution.py:278
  49.7 0.6 %copy.5 = f32[2,8,256]{2,1,0:T(8,128)} copy(f32[2,8,256]{2,1,0:T(8,128)S(1)} %shard_map.37) | data formatting | bytes 32768
Async XLA Ops:
  0.0 1.2 %copy-start = (bf16[2,32,8192]{2,1,0:T(8,128)(2,1)S(1)}, bf16[2,32,8192]{2,1,0:T(8,128)(2,1)}, u32[]{:S(2)}) copy-start(bf16[2,32,8192]{2,1,0:T(8,128)(2,1)} %teach_hbm.1) | copy-start | bytes 3145732
  1.2 1.2 %copy-start.1 = (bf16[2,32,8192]{2,1,0:T(8,128)(2,1)S(1)}, bf16[2,32,8192]{2,1,0:T(8,128)(2,1)}, u32[]{:S(2)}) copy-start(bf16[2,32,8192]{2,1,0:T(8,128)(2,1)} %stud_hbm.1) | copy-start | bytes 3145732
  2.5 0.7 %copy-start.2 = (s32[40]{0:T(128)S(1)}, s32[40]{0:T(128)}, u32[]{:S(2)}) copy-start(s32[40]{0:T(128)} %kept_ref.1) | copy-start | bytes 484

commit v3 on v2

--- a/solution.py
+++ b/solution.py
@@ -299,7 +299,7 @@
             dma, dma, dma, dma, dma((chunks,)), dma((chunks,)), dma, dma,
         ],
         compiler_params=pltpu.CompilerParams(
-            collective_id=0, has_side_effects=True, vmem_limit_bytes=48 * 2**20
+            collective_id=0, has_side_effects=True, vmem_limit_bytes=60 * 2**20
         ),
     )(kept_heads, teacher_query, student_query)
 

time: 50.5 us -> 49.2 us (0.974)
  local copies, waits for them, and re-layouts: 3.71 us -> 1.32 us
  Pallas kernels: 46.6 us -> 47.7 us
    unnamed x7 -> x1, local copies, waits for them, and re-layouts: 3.71 us -> 1.32 us
    pallas_call x1, Pallas kernels: 46.6 us -> 47.7 us  [shards(): pl.pallas_call(functools.partial(kernel, seq_n, head_n, rows, chunk), out...]
where the time goes in v3:
time: 49.2 us; the launch traced here: 49.1 us
  Pallas kernels  47.7 us (97%)
  local copies, waits for them, and re-layouts  1.32 us (3%)
    pallas_call x1, Pallas kernels, shards(): pl.pallas_call(functools.partial(kernel, seq_n, head_n, rows, chunk), out...  47.7 us
    unnamed x1, local copies, waits for them, and re-layouts  1.32 us

profile of v3, /device:TPU:1, one launch (start us, length us, event | category | flops | bytes accessed | tf_op | source)
XLA Modules:
  0.0 49.1 jit_solution(4913812498392576390)
XLA Ops:
  0.0 47.7 %shard_map.37 = f32[2,8,256]{2,1,0:T(8,128)} custom-call(s32[40]{0:T(128)} %kept_ref.1, bf16[2,32,8192]{2,1,0:T(8,128)(2,1)} %teach_hbm.1, bf16[2,32,8192]{2,1,0:T(8,128)(2,1)} %stud_hbm.1), custom_call_target="tpu_custom_call" | custom-call | tf_op jit(solution)/shard_map/pallas_call | solution.py:278
  47.7 1.3 %copy.5 = f32[2,8,256]{2,1,0:T(8,128)} copy(f32[2,8,256]{2,1,0:T(8,128)} %shard_map.37) | data formatting | bytes 32768

commit v4 on v3

--- a/solution.py
+++ b/solution.py
@@ -29,7 +29,7 @@
 
 
 ORDER = (1, 3, 2, 0)
-AHEAD = 4
+EARLY = 2
 
 
 def xor2(a, b):
@@ -73,15 +73,63 @@
         for h in heads_from_me:
             pl.semaphore_signal(barrier, inc=1, device_id=(s, h), device_id_type=MESH)
 
+    load_t = pltpu.make_async_copy(teach_hbm, teach_in, in_t)
+    load_t.start()
+
     @pl.loop(0, HEADS)
     def _(i):
         head = stud_hbm.at[:, :, pl.ds(pl.multiple_of(i * HD, HD), HD)]
         pltpu.make_async_copy(head, stud_in.at[i], in_sem).start()
 
-    load_t = pltpu.make_async_copy(teach_hbm, teach_in, in_t)
-    load_t.start()
-
-    sums[...] = jnp.zeros_like(sums)
+    load_t.wait()
+    pl.semaphore_wait(barrier, total - 1)
+
+    mine = pl.ds(pl.multiple_of(me * rows, rows), rows)
+
+    def teach_src(s, h):
+        r = h * 8 + lax.rem(s, 8)
+        return teach_in.at[lax.div(s, 8), :, pl.ds(pl.multiple_of(r * TREL, TREL), TREL)]
+
+    own_t = pltpu.make_async_copy(teach_src(seq_me, head_me), tea.at[mine], recv_t.at[my_chunk])
+    own_s = pltpu.make_async_copy(stud_out.at[me], packed.at[me], recv_s.at[my_chunk])
+    own_t.start()
+
+    x_at = [lax.rem(x_me + i, 4) for i in range(4)]
+    y_at = [lax.rem(y_me + i, 4) for i in range(4)]
+
+    def send_teach(s, h):
+        pltpu.make_async_remote_copy(
+            src_ref=teach_src(s, h), dst_ref=tea.at[mine], send_sem=send_t, recv_sem=recv_t.at[my_chunk],
+            device_id=(s, h), device_id_type=MESH,
+        ).start()
+
+    def send_stud(s, h):
+        pltpu.make_async_remote_copy(
+            src_ref=stud_out.at[s * head_n + h], dst_ref=packed.at[me], send_sem=send_s,
+            recv_sem=recv_s.at[my_chunk], device_id=(s, h), device_id_type=MESH,
+        ).start()
+
+    def send(step, *kinds):
+        chunk_of = [chunk_at(step, core) for core in range(2)]
+        for j in range(per_chunk):
+            core, x = j % 2, (j // 2) % 4
+            y = (x + j // 8) % 4
+            s = chunk_of[core] * 4 + x_at[x]
+            h = y_at[y] * 2 + core
+
+            def copies(s=s, h=h):
+                for kind in kinds:
+                    kind(s, h)
+
+            if x == 0 and y == 0:
+                pl.when((s != seq_me) | (h != head_me))(copies)
+            else:
+                copies()
+
+    @pl.loop(0, EARLY)
+    def _(step):
+        send(step, send_teach)
+
     pltpu.make_async_copy(stud_in, stud_in, in_sem).wait()
 
     lane = lax.broadcasted_iota(jnp.int32, (rows, HD), 1)
@@ -109,50 +157,17 @@
             stud_out[to, 1] = jnp.where(tile_lane < 64, v[1], pltpu.roll(v[3], 64, 1)).astype(BF)
             stud_out[to, 2] = rest.astype(BF)
 
-    load_t.wait()
-    pl.semaphore_wait(barrier, total - 1)
-
-    mine = pl.ds(pl.multiple_of(me * rows, rows), rows)
-
-    def teach_src(s, h):
-        r = h * 8 + lax.rem(s, 8)
-        return teach_in.at[lax.div(s, 8), :, pl.ds(pl.multiple_of(r * TREL, TREL), TREL)]
-
-    own_t = pltpu.make_async_copy(teach_src(seq_me, head_me), tea.at[mine], recv_t.at[my_chunk])
-    own_s = pltpu.make_async_copy(stud_out.at[me], packed.at[me], recv_s.at[my_chunk])
-    own_t.start()
     own_s.start()
 
-    x_at = [lax.rem(x_me + i, 4) for i in range(4)]
-    y_at = [lax.rem(y_me + i, 4) for i in range(4)]
-
-    def send(step):
-        chunk_of = [chunk_at(step, core) for core in range(2)]
-        for j in range(per_chunk):
-            core, x = j % 2, (j // 2) % 4
-            y = (x + j // 8) % 4
-            s = chunk_of[core] * 4 + x_at[x]
-            h = y_at[y] * 2 + core
-
-            def copies(s=s, h=h):
-                pltpu.make_async_remote_copy(
-                    src_ref=teach_src(s, h), dst_ref=tea.at[mine], send_sem=send_t, recv_sem=recv_t.at[my_chunk],
-                    device_id=(s, h), device_id_type=MESH,
-                ).start()
-                pltpu.make_async_remote_copy(
-                    src_ref=stud_out.at[s * head_n + h], dst_ref=packed.at[me], send_sem=send_s,
-                    recv_sem=recv_s.at[my_chunk], device_id=(s, h), device_id_type=MESH,
-                ).start()
-
-            if x == 0 and y == 0:
-                pl.when((s != seq_me) | (h != head_me))(copies)
-            else:
-                copies()
-
-    @pl.loop(0, AHEAD)
+    @pl.loop(0, EARLY)
     def _(step):
-        send(step)
-
+        send(step, send_stud)
+
+    @pl.loop(EARLY, chunks)
+    def _(step):
+        send(step, send_teach, send_stud)
+
+    sums[...] = jnp.zeros_like(sums)
     part = 256
     row_i = lax.broadcasted_iota(jnp.int32, (TREL, HD), 0)
     col_i = lax.broadcasted_iota(jnp.int32, (TREL, HD), 1)
@@ -205,10 +220,6 @@
         pltpu.make_async_copy(tea.at[here], tea.at[here], recv_t.at[c]).wait()
         from_c = pl.ds(pl.multiple_of(c * per_chunk, per_chunk), per_chunk)
         pltpu.make_async_copy(packed.at[from_c], packed.at[from_c], recv_s.at[c]).wait()
-
-        @pl.when(n + AHEAD < chunks)
-        def _():
-            send(n + AHEAD)
 
         a = tea[here].astype(F32)
         norm_t = jnp.dot((a * a).astype(BF), pick_t, preferred_element_type=F32)
@@ -237,23 +248,20 @@
         diagonal(c * chunk)
 
     each = positions // seq_n
-    for j in range(seq_n):
-        part = pl.ds(j * each, each)
+    for k in range(1, seq_n + 1):
+        to = lax.rem(seq_me + k, seq_n)
+        part = pl.ds(pl.multiple_of(to * each, each), each)
         total_t = jnp.sum(sums[0, :, part], axis=0, keepdims=True)
         total_s = jnp.sum(sums[1, :, part], axis=0, keepdims=True)
         cross = jnp.sum(sums[2, :, part], axis=0, keepdims=True)
-        rows_out[j] = (cross / total_t - jnp.log2(total_t) + jnp.log2(total_s)) * math.log(2.0)
-
-    own_o = pltpu.make_async_copy(rows_out.at[seq_me], rows_in.at[seq_me], recv_o)
-    own_o.start()
-
-    @pl.loop(1, seq_n)
-    def _(k):
-        s = lax.rem(seq_me + k, seq_n)
-        pltpu.make_async_remote_copy(
-            src_ref=rows_out.at[s], dst_ref=rows_in.at[seq_me], send_sem=send_o, recv_sem=recv_o,
-            device_id=(s, head_me), device_id_type=MESH,
-        ).start()
+        rows_out[to] = (cross / total_t - jnp.log2(total_t) + jnp.log2(total_s)) * math.log(2.0)
+        if k < seq_n:
+            pltpu.make_async_remote_copy(
+                src_ref=rows_out.at[to], dst_ref=rows_in.at[seq_me], send_sem=send_o, recv_sem=recv_o,
+                device_id=(to, head_me), device_id_type=MESH,
+            ).start()
+        else:
+            pltpu.make_async_copy(rows_out.at[to], rows_in.at[to], recv_o).start()
 
     pltpu.make_async_copy(rows_in, rows_in, recv_o).wait()
     out_ref[...] = rows_in[...].reshape(2, 8, each)

time: 49.2 us -> 46.7 us (0.949)
  Pallas kernels: 47.7 us -> 45.2 us
    pallas_call x1, Pallas kernels: 47.7 us -> 45.2 us  [shards(): pl.pallas_call(functools.partial(kernel, seq_n, head_n, rows, chunk), out...]
where the time goes in v4:
time: 46.7 us; the launch traced here: 46.6 us
  Pallas kernels  45.2 us (97%)
  local copies, waits for them, and re-layouts  1.32 us (3%)
    pallas_call x1, Pallas kernels, shards(): pl.pallas_call(functools.partial(kernel, seq_n, head_n, rows, chunk), out...  45.2 us
    unnamed x1, local copies, waits for them, and re-layouts  1.32 us

profile of v4, /device:TPU:1, one launch (start us, length us, event | category | flops | bytes accessed | tf_op | source)
XLA Modules:
  0.0 46.6 jit_solution(7301544425510405718)
XLA Ops:
  0.0 45.2 %shard_map.37 = f32[2,8,256]{2,1,0:T(8,128)} custom-call(s32[40]{0:T(128)} %kept_ref.1, bf16[2,32,8192]{2,1,0:T(8,128)(2,1)} %teach_hbm.1, bf16[2,32,8192]{2,1,0:T(8,128)(2,1)} %stud_hbm.1), custom_call_target="tpu_custom_call" | custom-call | tf_op jit(solution)/shard_map/pallas_call | solution.py:286
  45.2 1.3 %copy.5 = f32[2,8,256]{2,1,0:T(8,128)} copy(f32[2,8,256]{2,1,0:T(8,128)} %shard_map.37) | data formatting | bytes 32768

commit v5 on v4

--- a/solution.py
+++ b/solution.py
@@ -29,7 +29,7 @@
 
 
 ORDER = (1, 3, 2, 0)
-EARLY = 2
+EARLY = 3
 
 
 def xor2(a, b):
@@ -61,6 +61,9 @@
             code = jnp.where(step == i, ORDER[i], code)
         return xor2(xor2(my_chunk, code), 2 * core)
 
+    load_t = pltpu.make_async_copy(teach_hbm, teach_in, in_t)
+    load_t.start()
+
     barrier = pltpu.get_barrier_semaphore()
 
     heads_from_me = [lax.rem(head_me + i, head_n) for i in range(head_n)]
@@ -73,9 +76,6 @@
         for h in heads_from_me:
             pl.semaphore_signal(barrier, inc=1, device_id=(s, h), device_id_type=MESH)
 
-    load_t = pltpu.make_async_copy(teach_hbm, teach_in, in_t)
-    load_t.start()
-
     @pl.loop(0, HEADS)
     def _(i):
         head = stud_hbm.at[:, :, pl.ds(pl.multiple_of(i * HD, HD), HD)]
@@ -112,8 +112,8 @@
     def send(step, *kinds):
         chunk_of = [chunk_at(step, core) for core in range(2)]
         for j in range(per_chunk):
-            core, x = j % 2, (j // 2) % 4
-            y = (x + j // 8) % 4
+            core, x = j % 2, (1, 3, 2, 0)[(j // 2 + 2 * (j % 2)) % 4]
+            y = (x + (3, 1, 2, 0)[j // 8]) % 4
             s = chunk_of[core] * 4 + x_at[x]
             h = y_at[y] * 2 + core
 

time: 46.7 us -> 46.5 us (level)
  no operation moved by 1% of the time
where the time goes in v5:
time: 46.5 us; the launch traced here: 46.1 us
  Pallas kernels  44.8 us (96%)
  local copies, waits for them, and re-layouts  1.32 us (3%)
    pallas_call x1, Pallas kernels, shards(): pl.pallas_call(functools.partial(kernel, seq_n, head_n, rows, chunk), out...  44.8 us
    unnamed x1, local copies, waits for them, and re-layouts  1.32 us

profile of v5, /device:TPU:1, one launch (start us, length us, event | category | flops | bytes accessed | tf_op | source)
XLA Modules:
  0.0 46.1 jit_solution(10150906900959507674)
XLA Ops:
  0.0 44.8 %shard_map.37 = f32[2,8,256]{2,1,0:T(8,128)} custom-call(s32[40]{0:T(128)} %kept_ref.1, bf16[2,32,8192]{2,1,0:T(8,128)(2,1)} %teach_hbm.1, bf16[2,32,8192]{2,1,0:T(8,128)(2,1)} %stud_hbm.1), custom_call_target="tpu_custom_call" | custom-call | tf_op jit(solution)/shard_map/pallas_call | solution.py:286
  44.8 1.3 %copy.5 = f32[2,8,256]{2,1,0:T(8,128)} copy(f32[2,8,256]{2,1,0:T(8,128)} %shard_map.37) | data formatting | bytes 32768
